TPU v7x, 256 devices: a whole 4x4x8 slice. The times are simulated.
256 devices in a mesh: grp: 4 (over y), dev: 64 (over x, z, core).
Axes of the slice: x: 4, y: 4, z: 8, core: 2. Of those that a mesh axis runs over, the one named last changes fastest.
Arguments:
- x_rows: bfloat16 [32768, 8192], P(('grp', 'dev')), may hold values from -6 to 6
- dt_rows: bfloat16 [32768, 128], P(('grp', 'dev')), may hold values from 0.0004 to 0.56
- bc_rows: bfloat16 [32768, 256], P(('grp', 'dev')), may hold values from -2 to 2
- a_log: float32 [128], P('dev'), may hold values from -0.35 to 0.35
- d_skip: float32 [128], P('dev'), may hold values from 0.5 to 1.5
- state_pool: float32 [64, 128, 64, 128], P('grp', 'dev'), may hold values from -2 to 2
- owners: int32 [128], P('grp'), may hold values from 0 to 63
- queries: bfloat16 [32768, 4096], P(('grp', 'dev')), may hold values from -6 to 6
- new_kv: bfloat16 [32768, 2048], P(('grp', 'dev')), may hold values from -6 to 6
- page_pool: bfloat16 [2048, 16, 2048], P(('grp', 'dev')), may hold values from -6 to 6
- page_table: int32 [128, 64], P('grp'), may hold values from 0 to 511, as said below
- prefix_len: int32 [128], P('grp'), may hold values from 256 to 1024, as said below
Outputs:
- ssd_out: bfloat16 [32768, 8192], P('grp', 'dev')
- final_states: float32 [128, 128, 64, 128], P('grp', 'dev')
- attn_out: bfloat16 [32768, 4096], P(('grp', 'dev'))
Inputs may be any that keep to these rules, and one draw needn't show every extreme that they name: `page_table`: id // 8 is the index along dev of the device of the request's group that holds the page, id % 8 its place there; each row holds exactly 1 ids of every such device. `prefix_len`: the largest equals 1024.
All inputs are finite; a program needn't handle non-finite values.
Results may differ from a plain program's by a relative error of at most 0.0045.
Values may be sent and summed in bfloat16 or wider, within the bound.
A program may use at most 128 MiB of HBM per device.

v0:
```python
import math

import jax
import jax.numpy as jnp
from jax import lax
from jax.experimental import pallas as pl
from jax.experimental.pallas import tpu as pltpu
from jax.sharding import PartitionSpec as P

MESH = pl.DeviceIdType.MESH
F32, BF16 = jnp.float32, jnp.bfloat16
NX, NZ, NC, NG = 4, 8, 2, 4
NDEV = NX * NZ * NC
REQ = 32
TOK = 128
NEW = 2 * TOK
HEADS_CORE = 4
QPER = 4
PAGE = 16
HELD = 8
PARTS = 1
ROUTES = 9
PIECES = 4
PREFIX = 1024
HALF = HEADS_CORE * 128
QHALF = HEADS_CORE * QPER * 128
PHASES = 2
PER_PHASE = HEADS_CORE // PHASES
LOG2E = math.log2(math.e)
EXP2_SCALE = LOG2E / math.sqrt(128.0)
HIDDEN = -1e30

NT = (((1,), (1,)), ((), ()))
TN = (((0,), (0,)), ((), ()))


def dot(a, b, dims=(((1,), (0,)), ((), ())), precision=None):
    return lax.dot_general(a, b, dims, precision=precision, preferred_element_type=F32)


def kernel(
    owners,
    a_log,
    d_skip,
    prefix_len,
    table_in,
    dt_in,
    x_in,
    bc_in,
    pool_in,
    q_in,
    kv_in,
    pages_in,
    ssd_v,
    fin_v,
    attn_v,
    xbuf,
    dtbuf,
    bcbuf,
    states,
    pool_own,
    up_near,
    up_far,
    down_near,
    down_far,
    stage,
    kvbuf,
    qbuf,
    newbuf,
    obuf,
    by_req,
    dt_rows,
    dt_stage,
    slots_v,
    slots,
    bias,
    recv,
    send,
    ring_bc,
    ring_pg,
    recv_x,
    recv_bx,
    recv_c,
    out_sem,
):
    grp = lax.axis_index("grp")
    me = lax.axis_index("dev")
    myx, myz, myc = lax.div(me, NZ * NC), lax.rem(lax.div(me, NC), NZ), lax.rem(me, NC)
    other = me + 1 - 2 * myc

    def peer(step):
        x = lax.rem(myx + lax.div(step, NZ * NC), NX)
        z = lax.rem(myz + lax.div(step, NC), NZ)
        return (x * NZ + z) * NC + lax.rem(myc + step, NC)

    def remote(src, dst, send_sem, recv_sem, where):
        return pltpu.make_async_remote_copy(
            src_ref=src,
            dst_ref=dst,
            send_sem=send_sem,
            recv_sem=recv_sem,
            device_id=where,
            device_id_type=MESH,
        )

    def wait_for(ref, sem):
        pltpu.make_async_copy(ref, ref, sem).wait()

    R_DT, R_ST, R_Q, R_NK, R_BC, R_PG, R_KV, R_OUT = range(8)
    S_X, S_DT, S_ST, S_Q, S_NK, S_BC, S_PG, S_BX, S_KV, S_CORE, S_OUT = range(11)

    barrier = pltpu.get_barrier_semaphore()

    @pl.loop(1, NDEV)
    def _(step):
        pl.semaphore_signal(barrier, inc=1, device_id={"dev": peer(step)}, device_id_type=MESH)

    for dg in range(1, NG):
        pl.semaphore_signal(
            barrier, inc=1, device_id={"grp": (grp + dg) % NG}, device_id_type=MESH
        )

    pl.semaphore_wait(barrier, NDEV - 1 + NG - 1)

    def on_ring(dz):
        return lax.rem(myz + dz + NZ, NZ)

    def at(x, z, c):
        return {"dev": (x * NZ + z) * NC + c}

    def map_rows(side):
        return pl.ds(side * (TOK // 2), TOK // 2)

    def page_rows(part):
        return pl.ds(part * (HELD // PARTS), HELD // PARTS)

    ways = (1, -1)
    held = ((up_near, up_far), (down_near, down_far))

    def pass_maps(step, side, source, distance=1, rows=None):
        block = bcbuf.at[myx, myc, on_ring(-min(step - 1, 2) * ways[side])]
        if rows is not None:
            block = block.at[rows]
        remote(
            block if source is None else source,
            block,
            send.at[S_BC],
            ring_bc.at[side, step - 1],
            at(myx, on_ring(distance * ways[side]), myc),
        ).start()

    def pass_pages(step, side, part):
        source = pages_in if step == 1 else held[side][0]
        remote(
            source.at[page_rows(part)],
            held[side][step - 1].at[page_rows(part)],
            send.at[S_PG],
            ring_pg.at[side, step - 1, part],
            at(myx, on_ring(ways[side]), myc),
        ).start()

    for side in range(2):
        pass_maps(1, side, bc_in)
    for part in range(PARTS):
        for side in range(2):
            pass_pages(1, side, part)
    own_pages = pltpu.make_async_copy(pages_in, pool_own, recv.at[R_PG])
    own_pages.start()
    own_maps = pltpu.make_async_copy(bc_in, bcbuf.at[myx, myc, myz], recv.at[R_BC])
    own_maps.start()

    def send_x(dz, k):
        x = lax.rem(myx + lax.div(k, NC), NX)
        to = (x * NZ + lax.rem(myz + dz, NZ)) * NC + lax.rem(myc + k, NC)
        remote(
            x_in.at[:, pl.ds(pl.multiple_of(to * 128, 128), 128)],
            xbuf.at[myz, myx, myc],
            send.at[S_X],
            recv_x.at[dz],
            {"dev": to},
        ).start()

    pltpu.make_async_copy(
        x_in.at[:, pl.ds(pl.multiple_of(me * 128, 128), 128)],
        xbuf.at[myz, myx, myc],
        recv_x.at[0],
    ).start()

    @pl.loop(1, NX * NC)
    def _(k):
        send_x(0, k)

    holder, place = lax.shift_right_logical(table_in[...], 3), table_in[...] & (HELD - 1)
    lane = lax.broadcasted_iota(jnp.int32, (REQ, 128), 1)
    found = jnp.zeros((REQ, 128), jnp.int32)
    for z in range(NZ):
        line = (myx * NZ + z) * NC + myc
        here = jnp.sum(jnp.where(holder == line, place, 0), axis=1, keepdims=True)
        found = jnp.where(lane == z, here, found)
    slots_v[...] = found
    to_smem = pltpu.make_async_copy(slots_v, slots, out_sem.at[0])
    to_smem.start()

    by_head = dt_in[...].astype(F32).T
    for pair in range(NDEV):
        dt_stage[pair] = by_head[2 * pair : 2 * pair + 2]
    states[grp] = pool_in[...].astype(BF16)

    for dg in range(1, NG):
        remote(
            states.at[grp],
            states.at[grp],
            send.at[S_ST],
            recv.at[R_ST],
            {"grp": lax.rem(grp + dg, NG)},
        ).start()

    pltpu.make_async_copy(dt_stage.at[me], dtbuf.at[myz, myx, myc], recv.at[R_DT]).start()

    @pl.loop(1, NDEV)
    def _(step):
        to = peer(step)
        remote(
            dt_stage.at[to], dtbuf.at[myz, myx, myc], send.at[S_DT], recv.at[R_DT], {"dev": to}
        ).start()

    def send_both_ways(near):
        @pl.loop(0, 2 * NX * NC)
        def _(i):
            send_x(near + lax.rem(i, 2) * (NZ - 2 * near), lax.div(i, 2))

    def send_far():
        @pl.loop(0, NX * NC)
        def _(k):
            send_x(4, k)

    my_rows = pl.ds(pl.multiple_of(myc * TOK, TOK), TOK)

    def half(ref, start, width, core):
        return ref.at[:, pl.ds(pl.multiple_of(start + core * width, width), width)]

    pltpu.make_async_copy(half(q_in, 0, QHALF, myc), qbuf.at[my_rows], recv.at[R_Q]).start()
    remote(
        half(q_in, 0, QHALF, 1 - myc),
        qbuf.at[my_rows],
        send.at[S_Q],
        recv.at[R_Q],
        {"dev": other},
    ).start()
    for kv in range(2):
        pltpu.make_async_copy(
            half(kv_in, kv * 2 * HALF, HALF, myc), newbuf.at[kv, my_rows], recv.at[R_NK]
        ).start()
        remote(
            half(kv_in, kv * 2 * HALF, HALF, 1 - myc),
            newbuf.at[kv, my_rows],
            send.at[S_NK],
            recv.at[R_NK],
            {"dev": other},
        ).start()

    def spread_maps(z):
        block = bcbuf.at[myx, myc, z]
        for dx in range(1, NX):
            remote(
                block,
                block,
                send.at[S_BX],
                recv_bx.at[dx],
                at(lax.rem(myx + dx, NX), myz, myc),
            ).start()

    def spread_pages(place, pages, away, onward=0, cores=(0, 1)):
        z, target = on_ring(away), on_ring(onward)
        mine = kvbuf.at[:, :, myx, myc, z]

        @pl.loop(0, NX)
        def _(x):
            slot = slots[x * NZ + target, z]
            for kv in range(2):
                for c in cores:
                    for hh in range(HEADS_CORE):
                        col = ((kv * 2 + c) * HEADS_CORE + hh) * 128
                        stage[place, x, c, hh, kv] = pages[slot, :, col : col + 128]

        def pages_to(x, c):
            remote(
                stage.at[place, x, c], mine, send.at[S_KV], recv.at[R_KV], at(x, target, c)
            ).start()

        if onward == 0:
            pltpu.make_async_copy(stage.at[place, myx, myc], mine, recv.at[R_KV]).start()

            @pl.loop(1, NX * NC)
            def _(k):
                pages_to(lax.rem(myx + lax.div(k, NC), NX), lax.rem(myc + k, NC))
        elif len(cores) == 2:

            @pl.loop(0, NX * NC)
            def _(k):
                pages_to(lax.rem(myx + lax.div(k, NC), NX), lax.rem(myc + k, NC))
        else:

            @pl.loop(0, NX)
            def _(dx):
                pages_to(lax.rem(myx + dx, NX), cores[0])

    mine = lax.broadcasted_iota(jnp.int32, (REQ, NDEV), 0) == lax.div(me, NC)
    my_holders = jnp.sum(jnp.where(mine, holder.astype(F32), 0.0), axis=0, keepdims=True)
    block = lax.broadcasted_iota(jnp.int32, (NDEV, NDEV), 0)
    block_holder = (
        (block // (NC * NZ)) * (NC * NZ) + (block % NZ) * NC + (block // NZ) % NC
    ).astype(F32)
    entry = lax.broadcasted_iota(jnp.int32, (8, NDEV), 1).astype(F32)
    found_at = dot(entry, (my_holders == block_holder).astype(F32), NT)
    key = lax.broadcasted_iota(jnp.int32, (NDEV, PREFIX), 1)
    spread = (key // PAGE == lax.broadcasted_iota(jnp.int32, (NDEV, PREFIX), 0)).astype(F32)
    position = dot(found_at, spread) * PAGE + (
        lax.broadcasted_iota(jnp.int32, (8, PREFIX), 1) % PAGE
    ).astype(F32)
    length = jnp.full((8, PREFIX), prefix_len[lax.div(me, NC)]).astype(F32)
    bias[...] = jnp.where(position < length, 0.0, HIDDEN)

    to_smem.wait()
    own_maps.wait()
    spread_maps(myz)
    own_pages.wait()
    spread_pages(0, pool_own, 0)
    for step in (1, 2):
        for side in range(2):
            z = on_ring(-step * ways[side])
            wait_for(bcbuf.at[myx, myc, z], ring_bc.at[side, step - 1])
            pass_maps(step + 1, side, None)
            if step == 2:
                pass_maps(4, side, None, 2, map_rows(side))
        for part in range(PARTS):
            for side in range(2):
                wait_for(
                    held[side][step - 1].at[page_rows(part)], ring_pg.at[side, step - 1, part]
                )
                if step == 1:
                    pass_pages(2, side, part)
        for side in range(2):
            spread_maps(on_ring(-step * ways[side]))
        if step == 2:
            for side in range(2):
                spread_pages(5 + side, held[side][1], -2 * ways[side], 2 * ways[side], (side,))
            for side in range(2):
                spread_pages(7 + side, held[side][1], -2 * ways[side], ways[side])
        for side in range(2):
            spread_pages(2 * step - 1 + side, held[side][step - 1], -step * ways[side])

    for side in range(2):
        z = on_ring(-3 * ways[side])
        wait_for(bcbuf.at[myx, myc, z], ring_bc.at[side, 2])
        spread_maps(z)
    far = on_ring(4)
    for side in range(2):
        wait_for(bcbuf.at[myx, myc, far, map_rows(side)], ring_bc.at[side, 3])
    spread_maps(far)
    send_far()
    send_both_ways(3)

    def maps_to_other_core():
        for dx in range(NX):
            block = bcbuf.at[lax.rem(myx + NX - dx, NX), myc]
            if dx:
                wait_for(block, recv_bx.at[dx])
            remote(block, block, send.at[S_CORE], recv_c.at[dx], {"dev": other}).start()

    maps_to_other_core()
    send_both_ways(2)
    send_both_ways(1)
    wait_for(qbuf, recv.at[R_Q])
    wait_for(newbuf, recv.at[R_NK])
    wait_for(kvbuf, recv.at[R_KV])
    causal = lax.broadcasted_iota(jnp.int32, (NEW, NEW), 0) >= lax.broadcasted_iota(
        jnp.int32, (NEW, NEW), 1
    )
    for p in range(PHASES):
        @pl.loop(p * PER_PHASE * QPER, (p + 1) * PER_PHASE * QPER)
        def _(qh):
            h = lax.div(qh, QPER)
            head_cols = pl.ds(pl.multiple_of(h * 128, 128), 128)
            q = qbuf[:, pl.ds(pl.multiple_of(qh * 128, 128), 128)]
            keys = kvbuf[h, 0].reshape(PREFIX, 128)
            values = kvbuf[h, 1].reshape(PREFIX, 128)
            old = dot(q, keys, NT) + bias[0:1, :]
            new = jnp.where(causal, dot(q, newbuf[0, :, head_cols], NT), HIDDEN)
            top = jnp.maximum(
                jnp.max(old, axis=1, keepdims=True), jnp.max(new, axis=1, keepdims=True)
            )
            shift = top * EXP2_SCALE
            old = jnp.exp2(old * EXP2_SCALE - shift)
            new = jnp.exp2(new * EXP2_SCALE - shift)
            totals = jnp.sum(old, axis=1, keepdims=True) + jnp.sum(new, axis=1, keepdims=True)
            mixed = dot(old.astype(BF16), values) + dot(
                new.astype(BF16), newbuf[1, :, head_cols]
            )
            obuf[:, pl.ds(pl.multiple_of(qh * 128, 128), 128)] = (mixed / totals).astype(BF16)

        width = QHALF // PHASES
        src_cols = pl.ds(p * width, width)
        dst_cols = pl.ds(pl.multiple_of(myc * QHALF + p * width, width), width)
        pltpu.make_async_copy(
            obuf.at[my_rows, src_cols], attn_v.at[:, dst_cols], recv.at[R_OUT]
        ).start()
        remote(
            obuf.at[pl.ds(pl.multiple_of((1 - myc) * TOK, TOK), TOK), src_cols],
            attn_v.at[:, dst_cols],
            send.at[S_OUT],
            recv.at[R_OUT],
            {"dev": other},
        ).start()

    wait_for(dtbuf, recv.at[R_DT])
    wait_for(states.at[pl.ds(0, NG - 1)], recv.at[R_ST])
    for dx in range(NX):
        wait_for(bcbuf.at[lax.rem(myx + NX - dx, NX), 1 - myc], recv_c.at[dx])

    for r in range(REQ):
        for c in range(NC):
            dt_rows[2 * r : 2 * r + 2, c * TOK : (c + 1) * TOK] = dtbuf[r % NZ, r // NZ, c]
    odd_row = lax.broadcasted_iota(jnp.int32, (2 * REQ, NEW), 0) % 2 == 1
    rate = -jnp.exp(
        jnp.where(odd_row, jnp.full((2 * REQ, NEW), a_log[1]), jnp.full((2 * REQ, NEW), a_log[0]))
    )
    earlier = lax.broadcasted_iota(jnp.int32, (NEW, NEW), 0)
    later = lax.broadcasted_iota(jnp.int32, (NEW, NEW), 1)
    cumulative = dot(
        dt_rows[...] * (rate * LOG2E),
        (earlier <= later).astype(F32),
        precision=lax.Precision.HIGHEST,
    )
    less_step = cumulative - jnp.log2(dt_rows[...])
    for r in range(REQ):
        by_req[r, 0:2, :] = cumulative[2 * r : 2 * r + 2]
        by_req[r, 2:4, :] = less_step[2 * r : 2 * r + 2]

    second = lax.broadcasted_iota(jnp.int32, (1, 128), 1) >= 64
    skip = jnp.where(second, jnp.full((1, 128), d_skip[1]), jnp.full((1, 128), d_skip[0]))
    keep_second = second.astype(F32).astype(BF16)
    keep_first = (1.0 - second.astype(F32)).astype(BF16)
    low_half = lax.broadcasted_iota(jnp.int32, (128, 1), 0) < 64
    term = lax.broadcasted_iota(jnp.int32, (32, 4 * TOK), 0)
    lane = lax.broadcasted_iota(jnp.int32, (32, 4 * TOK), 1)
    wanted = jnp.where(lane < 2 * TOK, lane // TOK, 2 + lane // 64 - 4)
    chosen = ((term % 8 == wanted) & (term < 24)).astype(F32).astype(BF16)
    diagonal = lax.broadcasted_iota(jnp.int32, (TOK, TOK), 0) >= lax.broadcasted_iota(
        jnp.int32, (TOK, TOK), 1
    )

    def ssd_request(rx, rz):
        r = rx * NZ + rz
        x = jnp.concatenate([xbuf[rz, rx, 0], xbuf[rz, rx, 1]], axis=0)
        bc = jnp.concatenate([bcbuf[rx, 0, rz], bcbuf[rx, 1, rz]], axis=0)
        b, c = bc[:, :128], bc[:, 128:]
        kept = states[lax.div(owners[r], 16), lax.rem(owners[r], 16)]
        cum = by_req[r, 0:2, :]
        shifted = by_req[r, 2:4, :]
        last = cum[:, NEW - 1 :]
        rows = jnp.concatenate([cum, jnp.exp2(cum), jnp.exp2(last - shifted), cum], axis=0)
        high = rows.astype(BF16)
        left_over = rows - high.astype(F32)
        middle = left_over.astype(BF16)
        low = (left_over - middle.astype(F32)).astype(BF16)
        wide = dot(jnp.concatenate([high, middle, low, low], axis=0), chosen, TN)
        growth, gain = wide[:, 2 * TOK : 3 * TOK], wide[:, 3 * TOK :]
        inner_first = dot(c[:TOK], b[:TOK], NT)
        inner_second = dot(c[TOK:], b, NT)

        def decayed(h, inner, i, j):
            diff = (
                wide[i * TOK : (i + 1) * TOK, h * TOK : (h + 1) * TOK]
                - shifted[h : h + 1, j * TOK : (j + 1) * TOK]
            )
            if i == j:
                diff = jnp.where(diagonal, diff, HIDDEN)
            return (jnp.exp2(diff) * inner).astype(BF16)

        upper, lower = [], []
        for h in range(2):
            upper.append(decayed(h, inner_first, 0, 0))
            lower.append(decayed(h, inner_second[:, :TOK], 1, 0))
            lower.append(decayed(h, inner_second[:, TOK:], 1, 1))
        x_first = x * keep_first
        x_second = x * keep_second
        within = jnp.concatenate(
            [
                dot(
                    jnp.concatenate(upper, axis=1),
                    jnp.concatenate([x_first[:TOK], x_second[:TOK]], axis=0),
                ),
                dot(
                    jnp.concatenate(lower, axis=1), jnp.concatenate([x_first, x_second], axis=0)
                ),
            ],
            axis=0,
        )
        x_float = x.astype(F32)
        carried = growth * dot(c, kept, NT)
        ssd_v[pl.ds(pl.multiple_of(r * NEW, NEW), NEW), :] = (
            within + carried + skip * x_float
        ).astype(BF16)
        weighted = (x_float * gain).astype(BF16)
        total = jnp.exp2(last)
        left = jnp.where(
            low_half,
            jnp.broadcast_to(total[0:1], (128, 1)),
            jnp.broadcast_to(total[1:2], (128, 1)),
        )
        fin_v[r] = dot(weighted, b, TN) + left * kept.astype(F32)

    @pl.loop(0, NZ)
    def _(i):
        j = lax.rem(i + NZ - 1, NZ)
        odd = lax.rem(j, 2)
        dz = 4 + (1 - odd) * lax.div(j, 2) - odd * lax.div(j + 1, 2)
        rz = lax.rem(myz + NZ - dz, NZ)
        wait_for(xbuf.at[rz], recv_x.at[dz])

        for rx in range(NX):
            ssd_request(rx, rz)

    wait_for(attn_v, recv.at[R_OUT])
    wait_for(xbuf.at[pl.ds(0, NZ - 1)], send.at[S_X])
    wait_for(xbuf.at[0, pl.ds(0, NX - 1)], send.at[S_X])
    wait_for(xbuf.at[0, 0, 0], send.at[S_X])
    wait_for(dtbuf.at[pl.ds(0, NZ - 1)], send.at[S_DT])
    wait_for(dtbuf.at[0, pl.ds(0, NX - 1)], send.at[S_DT])
    wait_for(dtbuf.at[0, 0, 0], send.at[S_DT])
    wait_for(states.at[pl.ds(0, NG - 1)], send.at[S_ST])
    wait_for(qbuf.at[pl.ds(0, TOK)], send.at[S_Q])
    wait_for(newbuf.at[0], send.at[S_NK])
    wait_for(bcbuf.at[0, 0, pl.ds(0, NZ - 1)], send.at[S_BC])
    for pages in held[0] + held[1]:
        wait_for(pages, send.at[S_PG])
    wait_for(bcbuf.at[pl.ds(0, NX - 1), 0], send.at[S_BX])
    wait_for(bcbuf.at[:, 0], send.at[S_CORE])
    wait_for(obuf.at[pl.ds(0, TOK)], send.at[S_OUT])
    wait_for(stage.at[pl.ds(0, 7)], send.at[S_KV])
    wait_for(stage.at[0, 0], send.at[S_KV])
    wait_for(stage.at[0, 0, 0], send.at[S_KV])


def hand_over(*refs):
    sources, targets, sem = refs[:3], refs[3:6], refs[6]
    for i in range(3):
        rows = sources[i].shape[0] // PIECES
        for part in range(PIECES):
            piece = pl.ds(part * rows, rows)
            pltpu.make_async_copy(sources[i].at[piece], targets[i].at[piece], sem.at[i]).start()
    for i in range(3):
        pltpu.make_async_copy(sources[i], targets[i], sem.at[i]).wait()


def on_device(
    x_rows,
    dt_rows,
    bc_rows,
    a_log,
    d_skip,
    state_pool,
    owners,
    queries,
    new_kv,
    page_pool,
    page_table,
    prefix_len,
):
    smem = pl.BlockSpec(memory_space=pltpu.SMEM)
    vmem = pl.BlockSpec(memory_space=pltpu.VMEM)
    hbm = pl.BlockSpec(memory_space=pl.ANY)
    dma = pltpu.SemaphoreType.DMA
    ssd_out, finals, attn_out = pl.pallas_call(
        kernel,
        out_shape=(
            pltpu.VMEM((REQ * NEW, 128), BF16),
            pltpu.VMEM((REQ, 128, 128), F32),
            pltpu.VMEM((TOK, 2 * QHALF), BF16),
        ),
        in_specs=[smem] * 4 + [vmem, vmem, hbm, hbm, vmem, hbm, hbm, hbm],
        out_specs=(vmem, vmem, vmem),
        scratch_shapes=[
            pltpu.VMEM((NZ, NX, NC, TOK, 128), BF16),
            pltpu.VMEM((NZ, NX, NC, 2, TOK), F32),
            pltpu.VMEM((NX, NC, NZ, TOK, 256), BF16),
            pltpu.VMEM((NG, 16, 128, 128), BF16),
            *[pltpu.VMEM((HELD, PAGE, 4 * HALF), BF16)] * 5,
            pltpu.VMEM((ROUTES, NX, NC, HEADS_CORE, 2, PAGE, 128), BF16),
            pltpu.VMEM((HEADS_CORE, 2, NX, NC, NZ, PAGE, 128), BF16),
            pltpu.VMEM((NEW, QHALF), BF16),
            pltpu.VMEM((2, NEW, HALF), BF16),
            pltpu.VMEM((NEW, QHALF), BF16),
            pltpu.VMEM((REQ, 8, NEW), F32),
            pltpu.VMEM((2 * REQ, NEW), F32),
            pltpu.VMEM((NDEV, 2, TOK), F32),
            pltpu.VMEM((REQ, 128), jnp.int32),
            pltpu.SMEM((REQ, 128), jnp.int32),
            pltpu.VMEM((8, PREFIX), F32),
            dma((8,)),
            dma((11,)),
            dma((2, 4)),
            dma((2, 2, PARTS)),
            dma((NZ,)),
            dma((NX,)),
            dma((NX,)),
            dma((1,)),
        ],
        compiler_params=pltpu.CompilerParams(
            collective_id=0, has_side_effects=True, vmem_limit_bytes=54 * 1024 * 1024
        ),
    )(
        owners,
        a_log,
        d_skip,
        prefix_len,
        page_table,
        dt_rows,
        x_rows,
        bc_rows,
        state_pool.reshape(16, 128, 128),
        queries,
        new_kv,
        page_pool,
    )
    outs = (ssd_out, finals, attn_out)
    ssd_out, finals, attn_out = pl.pallas_call(
        hand_over,
        out_shape=tuple(jax.ShapeDtypeStruct(a.shape, a.dtype) for a in outs),
        in_specs=[vmem] * 3,
        out_specs=(hbm,) * 3,
        scratch_shapes=[dma((3,))],
        compiler_params=pltpu.CompilerParams(vmem_limit_bytes=40 * 1024 * 1024),
    )(*outs)
    return ssd_out, finals.reshape(REQ, 2, 64, 128), attn_out


def solution(mesh):
    return jax.shard_map(
        on_device,
        mesh=mesh,
        in_specs=(
            P(("grp", "dev"), None),
            P(("grp", "dev"), None),
            P(("grp", "dev"), None),
            P("dev"),
            P("dev"),
            P("grp", "dev", None, None),
            P("grp"),
            P(("grp", "dev"), None),
            P(("grp", "dev"), None),
            P(("grp", "dev"), None, None),
            P("grp", None),
            P("grp"),
        ),
        out_specs=(P("grp", "dev"), P("grp", "dev", None, None), P(("grp", "dev"), None)),
        check_vma=False,
    )
```

profile of v0, /device:TPU:1, one launch (start us, length us, event | category | flops | bytes accessed | tf_op | source)
XLA Modules:
  0.0 108.1 jit_solution(17659789998145849186)
XLA Ops:
  0.6 105.1 %shard_map.139 = (bf16[8192,128]{1,0:T(8,128)(2,1)S(1)}, f32[32,128,128]{2,1,0:T(8,128)S(1)}, bf16[128,4096]{1,0:T(8,128)(2,1)S(1)}) custom-call(s32[32]{0:T(128)} %owners.1, f32[2]{0:T(128)} %a_log.1, f32[2]{0:T(128)} %d_skip.1, s32[32]{0:T(128)} %prefix_len.1, s32[32,64]{1,0:T(8,128)} %table_in.1, bf16[128,128]{1,0:T(8,128)(2,1)} %dt_in.1, ...), custom_call_target="tpu_custom_call" | custom-call | tf_op jit(solution)/shard_map/pallas_call | solution.py:575
  105.7 2.3 %shard_map.140 = (bf16[8192,128]{1,0:T(8,128)(2,1)}, f32[32,128,128]{2,1,0:T(8,128)}, bf16[128,4096]{1,0:T(8,128)(2,1)}) custom-call(bf16[8192,128]{1,0:T(8,128)(2,1)S(1)} %get-tuple-element.9.refs_0_, f32[32,128,128]{2,1,0:T(8,128)S(1)} %get-tuple-element.10.refs_1_, bf16[128,4096]{1,0:T(8,128)(2,1)S(1)} %get-tuple-element.11.refs_2_), custom_call_target="tpu_custom_call" | custom-call | tf_op jit(solution)/shard_map/pallas_call | solution.py:628
where the time goes:
time: 108 us
  Pallas kernels  107 us (99%)
    pallas_call x1, Pallas kernels, on_device(): pl.pallas_call(kernel, out_shape=(pltpu.VMEM((REQ * NEW, 128), BF16), plt...  105 us
    pallas_call x1, Pallas kernels, on_device(): pl.pallas_call(hand_over, out_shape=tuple((jax.ShapeDtypeStruct(a.shape,...  2.35 us

commit v1 on v0

--- a/solution.py
+++ b/solution.py
@@ -20,7 +20,6 @@
 HELD = 8
 PARTS = 1
 ROUTES = 9
-PIECES = 4
 PREFIX = 1024
 HALF = HEADS_CORE * 128
 QHALF = HEADS_CORE * QPER * 128
@@ -36,6 +35,83 @@
 
 def dot(a, b, dims=(((1,), (0,)), ((), ())), precision=None):
     return lax.dot_general(a, b, dims, precision=precision, preferred_element_type=F32)
+
+
+def ssd_constants(d_skip):
+    second = lax.broadcasted_iota(jnp.int32, (1, 128), 1) >= 64
+    skip = jnp.where(second, jnp.full((1, 128), d_skip[1]), jnp.full((1, 128), d_skip[0]))
+    keep_second = second.astype(F32).astype(BF16)
+    keep_first = (1.0 - second.astype(F32)).astype(BF16)
+    low_half = lax.broadcasted_iota(jnp.int32, (128, 1), 0) < 64
+    term = lax.broadcasted_iota(jnp.int32, (32, 4 * TOK), 0)
+    lane = lax.broadcasted_iota(jnp.int32, (32, 4 * TOK), 1)
+    wanted = jnp.where(lane < 2 * TOK, lane // TOK, 2 + lane // 64 - 4)
+    chosen = ((term % 8 == wanted) & (term < 24)).astype(F32).astype(BF16)
+    diagonal = lax.broadcasted_iota(jnp.int32, (TOK, TOK), 0) >= lax.broadcasted_iota(
+        jnp.int32, (TOK, TOK), 1
+    )
+    return second, skip, keep_first, keep_second, low_half, diagonal, chosen
+
+
+def ssd_request(consts, by_req, xbuf, bcbuf, states, owners, rx, rz):
+    second, skip, keep_first, keep_second, low_half, diagonal, chosen = consts
+    r = rx * NZ + rz
+    x = jnp.concatenate([xbuf[rz, rx, 0], xbuf[rz, rx, 1]], axis=0)
+    bc = jnp.concatenate([bcbuf[rx, 0, rz], bcbuf[rx, 1, rz]], axis=0)
+    b, c = bc[:, :128], bc[:, 128:]
+    kept = states[lax.div(owners[r], 16), lax.rem(owners[r], 16)]
+    cum = by_req[r, 0:2, :]
+    shifted = by_req[r, 2:4, :]
+    last = cum[:, NEW - 1 :]
+    rows = jnp.concatenate([cum, jnp.exp2(cum), jnp.exp2(last - shifted), cum], axis=0)
+    high = rows.astype(BF16)
+    left_over = rows - high.astype(F32)
+    middle = left_over.astype(BF16)
+    low = (left_over - middle.astype(F32)).astype(BF16)
+    wide = dot(jnp.concatenate([high, middle, low, low], axis=0), chosen, TN)
+    growth, gain = wide[:, 2 * TOK : 3 * TOK], wide[:, 3 * TOK :]
+    inner_first = dot(c[:TOK], b[:TOK], NT)
+    inner_second = dot(c[TOK:], b, NT)
+
+    def decayed(h, inner, i, j):
+        diff = (
+            wide[i * TOK : (i + 1) * TOK, h * TOK : (h + 1) * TOK]
+            - shifted[h : h + 1, j * TOK : (j + 1) * TOK]
+        )
+        if i == j:
+            diff = jnp.where(diagonal, diff, HIDDEN)
+        return (jnp.exp2(diff) * inner).astype(BF16)
+
+    upper, lower = [], []
+    for h in range(2):
+        upper.append(decayed(h, inner_first, 0, 0))
+        lower.append(decayed(h, inner_second[:, :TOK], 1, 0))
+        lower.append(decayed(h, inner_second[:, TOK:], 1, 1))
+    x_first = x * keep_first
+    x_second = x * keep_second
+    within = jnp.concatenate(
+        [
+            dot(
+                jnp.concatenate(upper, axis=1),
+                jnp.concatenate([x_first[:TOK], x_second[:TOK]], axis=0),
+            ),
+            dot(
+                jnp.concatenate(lower, axis=1), jnp.concatenate([x_first, x_second], axis=0)
+            ),
+        ],
+        axis=0,
+    )
+    x_float = x.astype(F32)
+    carried = growth * dot(c, kept, NT)
+    mixed = (within + carried + skip * x_float).astype(BF16)
+    weighted = (x_float * gain).astype(BF16)
+    total = jnp.exp2(last)
+    left = jnp.where(
+        low_half,
+        jnp.broadcast_to(total[0:1], (128, 1)),
+        jnp.broadcast_to(total[1:2], (128, 1)),
+    )
+    return mixed, dot(weighted, b, TN) + left * kept.astype(F32)
 
 
 def kernel(
@@ -55,9 +131,10 @@
     fin_v,
     attn_v,
     xbuf,
-    dtbuf,
     bcbuf,
     states,
+    by_req,
+    dtbuf,
     pool_own,
     up_near,
     up_far,
@@ -68,7 +145,6 @@
     qbuf,
     newbuf,
     obuf,
-    by_req,
     dt_rows,
     dt_stage,
     slots_v,
@@ -111,9 +187,14 @@
 
     barrier = pltpu.get_barrier_semaphore()
 
-    @pl.loop(1, NDEV)
+    @pl.loop(1, NDEV, unroll=9)
     def _(step):
-        pl.semaphore_signal(barrier, inc=1, device_id={"dev": peer(step)}, device_id_type=MESH)
+        pl.semaphore_signal(
+            barrier,
+            inc=1,
+            device_id={"dev": lax.rem(me + step, NDEV)},
+            device_id_type=MESH,
+        )
 
     for dg in range(1, NG):
         pl.semaphore_signal(
@@ -437,90 +518,25 @@
         by_req[r, 0:2, :] = cumulative[2 * r : 2 * r + 2]
         by_req[r, 2:4, :] = less_step[2 * r : 2 * r + 2]
 
-    second = lax.broadcasted_iota(jnp.int32, (1, 128), 1) >= 64
-    skip = jnp.where(second, jnp.full((1, 128), d_skip[1]), jnp.full((1, 128), d_skip[0]))
-    keep_second = second.astype(F32).astype(BF16)
-    keep_first = (1.0 - second.astype(F32)).astype(BF16)
-    low_half = lax.broadcasted_iota(jnp.int32, (128, 1), 0) < 64
-    term = lax.broadcasted_iota(jnp.int32, (32, 4 * TOK), 0)
-    lane = lax.broadcasted_iota(jnp.int32, (32, 4 * TOK), 1)
-    wanted = jnp.where(lane < 2 * TOK, lane // TOK, 2 + lane // 64 - 4)
-    chosen = ((term % 8 == wanted) & (term < 24)).astype(F32).astype(BF16)
-    diagonal = lax.broadcasted_iota(jnp.int32, (TOK, TOK), 0) >= lax.broadcasted_iota(
-        jnp.int32, (TOK, TOK), 1
-    )
-
-    def ssd_request(rx, rz):
-        r = rx * NZ + rz
-        x = jnp.concatenate([xbuf[rz, rx, 0], xbuf[rz, rx, 1]], axis=0)
-        bc = jnp.concatenate([bcbuf[rx, 0, rz], bcbuf[rx, 1, rz]], axis=0)
-        b, c = bc[:, :128], bc[:, 128:]
-        kept = states[lax.div(owners[r], 16), lax.rem(owners[r], 16)]
-        cum = by_req[r, 0:2, :]
-        shifted = by_req[r, 2:4, :]
-        last = cum[:, NEW - 1 :]
-        rows = jnp.concatenate([cum, jnp.exp2(cum), jnp.exp2(last - shifted), cum], axis=0)
-        high = rows.astype(BF16)
-        left_over = rows - high.astype(F32)
-        middle = left_over.astype(BF16)
-        low = (left_over - middle.astype(F32)).astype(BF16)
-        wide = dot(jnp.concatenate([high, middle, low, low], axis=0), chosen, TN)
-        growth, gain = wide[:, 2 * TOK : 3 * TOK], wide[:, 3 * TOK :]
-        inner_first = dot(c[:TOK], b[:TOK], NT)
-        inner_second = dot(c[TOK:], b, NT)
-
-        def decayed(h, inner, i, j):
-            diff = (
-                wide[i * TOK : (i + 1) * TOK, h * TOK : (h + 1) * TOK]
-                - shifted[h : h + 1, j * TOK : (j + 1) * TOK]
-            )
-            if i == j:
-                diff = jnp.where(diagonal, diff, HIDDEN)
-            return (jnp.exp2(diff) * inner).astype(BF16)
-
-        upper, lower = [], []
-        for h in range(2):
-            upper.append(decayed(h, inner_first, 0, 0))
-            lower.append(decayed(h, inner_second[:, :TOK], 1, 0))
-            lower.append(decayed(h, inner_second[:, TOK:], 1, 1))
-        x_first = x * keep_first
-        x_second = x * keep_second
-        within = jnp.concatenate(
-            [
-                dot(
-                    jnp.concatenate(upper, axis=1),
-                    jnp.concatenate([x_first[:TOK], x_second[:TOK]], axis=0),
-                ),
-                dot(
-                    jnp.concatenate(lower, axis=1), jnp.concatenate([x_first, x_second], axis=0)
-                ),
-            ],
-            axis=0,
-        )
-        x_float = x.astype(F32)
-        carried = growth * dot(c, kept, NT)
-        ssd_v[pl.ds(pl.multiple_of(r * NEW, NEW), NEW), :] = (
-            within + carried + skip * x_float
-        ).astype(BF16)
-        weighted = (x_float * gain).astype(BF16)
-        total = jnp.exp2(last)
-        left = jnp.where(
-            low_half,
-            jnp.broadcast_to(total[0:1], (128, 1)),
-            jnp.broadcast_to(total[1:2], (128, 1)),
-        )
-        fin_v[r] = dot(weighted, b, TN) + left * kept.astype(F32)
-
-    @pl.loop(0, NZ)
+    consts = ssd_constants(d_skip)
+
+    @pl.loop(0, NZ - 2)
     def _(i):
-        j = lax.rem(i + NZ - 1, NZ)
+        j = lax.rem(i + NZ - 3, NZ - 2)
         odd = lax.rem(j, 2)
         dz = 4 + (1 - odd) * lax.div(j, 2) - odd * lax.div(j + 1, 2)
+        dz = dz * lax.div(i + NZ - 1, NZ)
         rz = lax.rem(myz + NZ - dz, NZ)
         wait_for(xbuf.at[rz], recv_x.at[dz])
-
         for rx in range(NX):
-            ssd_request(rx, rz)
+            r = rx * NZ + rz
+            rows = pl.ds(pl.multiple_of(r * NEW, NEW), NEW)
+            ssd_v[rows, :], fin_v[r] = ssd_request(
+                consts, by_req, xbuf, bcbuf, states, owners, rx, rz
+            )
+
+    for dz in (1, NZ - 1):
+        wait_for(xbuf.at[lax.rem(myz + NZ - dz, NZ)], recv_x.at[dz])
 
     wait_for(attn_v, recv.at[R_OUT])
     wait_for(xbuf.at[pl.ds(0, NZ - 1)], send.at[S_X])
@@ -543,15 +559,59 @@
     wait_for(stage.at[0, 0, 0], send.at[S_KV])
 
 
-def hand_over(*refs):
-    sources, targets, sem = refs[:3], refs[3:6], refs[6]
-    for i in range(3):
-        rows = sources[i].shape[0] // PIECES
-        for part in range(PIECES):
-            piece = pl.ds(part * rows, rows)
-            pltpu.make_async_copy(sources[i].at[piece], targets[i].at[piece], sem.at[i]).start()
-    for i in range(3):
-        pltpu.make_async_copy(sources[i], targets[i], sem.at[i]).wait()
+def hand_over(
+    owners,
+    d_skip,
+    ssd_v,
+    fin_v,
+    attn_v,
+    xbuf,
+    bcbuf,
+    states,
+    by_req,
+    ssd_out,
+    fin_out,
+    attn_out,
+    ssd_last,
+    fin_last,
+    sem,
+):
+    myz = lax.rem(lax.div(lax.axis_index("dev"), NC), NZ)
+
+    def rows_of(r):
+        return pl.ds(pl.multiple_of(r * NEW, NEW), NEW)
+
+    def write(ssd, fin, r):
+        pltpu.make_async_copy(ssd, ssd_out.at[rows_of(r)], sem.at[0]).start()
+        pltpu.make_async_copy(fin, fin_out.at[r], sem.at[1]).start()
+
+    pltpu.make_async_copy(attn_v, attn_out, sem.at[2]).start()
+
+    @pl.loop(0, NZ - 3)
+    def _(i):
+        for rx in range(NX):
+            r = rx * NZ + lax.rem(myz + 2 + i, NZ)
+            write(ssd_v.at[rows_of(r)], fin_v.at[r], r)
+
+    for rx in range(NX):
+        r = rx * NZ + myz
+        write(ssd_v.at[rows_of(r)], fin_v.at[r], r)
+
+    consts = ssd_constants(d_skip)
+
+    @pl.loop(0, 2)
+    def _(side):
+        rz = lax.rem(myz + NZ - 1 + 2 * side, NZ)
+        for rx in range(NX):
+            ssd_last[side, rx], fin_last[side, rx] = ssd_request(
+                consts, by_req, xbuf, bcbuf, states, owners, rx, rz
+            )
+        for rx in range(NX):
+            write(ssd_last.at[side, rx], fin_last.at[side, rx], rx * NZ + rz)
+
+    pltpu.make_async_copy(ssd_out, ssd_out, sem.at[0]).wait()
+    pltpu.make_async_copy(fin_out, fin_out, sem.at[1]).wait()
+    pltpu.make_async_copy(attn_v, attn_out, sem.at[2]).wait()
 
 
 def on_device(
@@ -572,27 +632,27 @@
     vmem = pl.BlockSpec(memory_space=pltpu.VMEM)
     hbm = pl.BlockSpec(memory_space=pl.ANY)
     dma = pltpu.SemaphoreType.DMA
-    ssd_out, finals, attn_out = pl.pallas_call(
+    left = pl.pallas_call(
         kernel,
         out_shape=(
             pltpu.VMEM((REQ * NEW, 128), BF16),
             pltpu.VMEM((REQ, 128, 128), F32),
             pltpu.VMEM((TOK, 2 * QHALF), BF16),
+            pltpu.VMEM((NZ, NX, NC, TOK, 128), BF16),
+            pltpu.VMEM((NX, NC, NZ, TOK, 256), BF16),
+            pltpu.VMEM((NG, 16, 128, 128), BF16),
+            pltpu.VMEM((REQ, 8, NEW), F32),
         ),
         in_specs=[smem] * 4 + [vmem, vmem, hbm, hbm, vmem, hbm, hbm, hbm],
-        out_specs=(vmem, vmem, vmem),
+        out_specs=(vmem,) * 7,
         scratch_shapes=[
-            pltpu.VMEM((NZ, NX, NC, TOK, 128), BF16),
             pltpu.VMEM((NZ, NX, NC, 2, TOK), F32),
-            pltpu.VMEM((NX, NC, NZ, TOK, 256), BF16),
-            pltpu.VMEM((NG, 16, 128, 128), BF16),
             *[pltpu.VMEM((HELD, PAGE, 4 * HALF), BF16)] * 5,
             pltpu.VMEM((ROUTES, NX, NC, HEADS_CORE, 2, PAGE, 128), BF16),
             pltpu.VMEM((HEADS_CORE, 2, NX, NC, NZ, PAGE, 128), BF16),
             pltpu.VMEM((NEW, QHALF), BF16),
             pltpu.VMEM((2, NEW, HALF), BF16),
             pltpu.VMEM((NEW, QHALF), BF16),
-            pltpu.VMEM((REQ, 8, NEW), F32),
             pltpu.VMEM((2 * REQ, NEW), F32),
             pltpu.VMEM((NDEV, 2, TOK), F32),
             pltpu.VMEM((REQ, 128), jnp.int32),
@@ -608,7 +668,7 @@
             dma((1,)),
         ],
         compiler_params=pltpu.CompilerParams(
-            collective_id=0, has_side_effects=True, vmem_limit_bytes=54 * 1024 * 1024
+            collective_id=0, has_side_effects=True, vmem_limit_bytes=46 * 1024 * 1024
         ),
     )(
         owners,
@@ -624,15 +684,18 @@
         new_kv,
         page_pool,
     )
-    outs = (ssd_out, finals, attn_out)
     ssd_out, finals, attn_out = pl.pallas_call(
         hand_over,
-        out_shape=tuple(jax.ShapeDtypeStruct(a.shape, a.dtype) for a in outs),
-        in_specs=[vmem] * 3,
+        out_shape=tuple(jax.ShapeDtypeStruct(a.shape, a.dtype) for a in left[:3]),
+        in_specs=[smem] * 2 + [vmem] * 7,
         out_specs=(hbm,) * 3,
-        scratch_shapes=[dma((3,))],
-        compiler_params=pltpu.CompilerParams(vmem_limit_bytes=40 * 1024 * 1024),
-    )(*outs)
+        scratch_shapes=[
+            pltpu.VMEM((2, NX, NEW, 128), BF16),
+            pltpu.VMEM((2, NX, 128, 128), F32),
+            dma((3,)),
+        ],
+        compiler_params=pltpu.CompilerParams(vmem_limit_bytes=16 * 1024 * 1024),
+    )(owners, d_skip, *left)
     return ssd_out, finals.reshape(REQ, 2, 64, 128), attn_out
 
 

time: 108 us -> 108 us (level)
    pallas_call x1, Pallas kernels: 105 us -> 102 us  [on_device(): pl.pallas_call(kernel, out_shape=(pltpu.VMEM((REQ * NEW, 128), BF16), plt...]
    pallas_call x1, Pallas kernels: 2.35 us -> 4.36 us  [on_device(): pl.pallas_call(hand_over, out_shape=tuple((jax.ShapeDtypeStruct(a.shape,...]
where the time goes in v1:
time: 108 us; the launch traced here: 107 us
  Pallas kernels  107 us (99%)
    pallas_call x1, Pallas kernels, on_device(): pl.pallas_call(kernel, out_shape=(pltpu.VMEM((REQ * NEW, 128), BF16), plt...  102 us
    pallas_call x1, Pallas kernels, on_device(): pl.pallas_call(hand_over, out_shape=tuple((jax.ShapeDtypeStruct(a.shape,...  4.36 us

profile of v1, /device:TPU:1, one launch (start us, length us, event | category | flops | bytes accessed | tf_op | source)
XLA Modules:
  0.0 107.5 jit_solution(979336058592946054)
XLA Ops:
  0.6 0.0 copy-start
  0.6 0.0 copy-start.1
  0.7 102.4 %shard_map.139 = (bf16[8192,128]{1,0:T(8,128)(2,1)S(1)}, f32[32,128,128]{2,1,0:T(8,128)S(1)}, bf16[128,4096]{1,0:T(8,128)(2,1)S(1)}, bf16[8,4,2,128,128]{4,3,2,1...) custom-call(s32[32]{0:T(128)} %owners.3, f32[2]{0:T(128)} %a_log.1, ...), custom_call_target="tpu_custom_call" | custom-call | tf_op jit(solution)/shard_map/pallas_call | solution.py:635
  103.1 0.0 copy-done
  103.1 0.0 copy-done.1
  103.1 4.4 %shard_map.140 = (bf16[8192,128]{1,0:T(8,128)(2,1)}, f32[32,128,128]{2,1,0:T(8,128)}, bf16[128,4096]{1,0:T(8,128)(2,1)}) custom-call(s32[32]{0:T(128)S(1)} %copy-done, f32[2]{0:T(128)S(1)} %copy-done.1, bf16[8192,128]{1,0:T(8,128)(2,1)S(1)} %get-tuple-element.13.ssd_v, f32[32,128,128]{2,1,0:T(8,128)S(1)} %get-tuple-element.14.fin_v, ...), custom_call_target="tpu_custom_call" | custom-call | tf_op jit(solution)/shard_map/pallas_call | solution.py:687
Async XLA Ops:
  0.6 102.5 %copy-start = (s32[32]{0:T(128)S(1)}, s32[32]{0:T(128)}, u32[]{:S(2)}) copy-start(s32[32]{0:T(128)} %owners.3) | copy-start | bytes 388
  0.6 102.5 %copy-start.1 = (f32[2]{0:T(128)S(1)}, f32[2]{0:T(128)}, u32[]{:S(2)}) copy-start(f32[2]{0:T(128)} %d_skip.3) | copy-start | bytes 28

commit v2 on v1

--- a/solution.py
+++ b/solution.py
@@ -298,12 +298,6 @@
 
     pltpu.make_async_copy(dt_stage.at[me], dtbuf.at[myz, myx, myc], recv.at[R_DT]).start()
 
-    @pl.loop(1, NDEV)
-    def _(step):
-        to = peer(step)
-        remote(
-            dt_stage.at[to], dtbuf.at[myz, myx, myc], send.at[S_DT], recv.at[R_DT], {"dev": to}
-        ).start()
 
     def send_both_ways(near):
         @pl.loop(0, 2 * NX * NC)
@@ -355,7 +349,7 @@
         z, target = on_ring(away), on_ring(onward)
         mine = kvbuf.at[:, :, myx, myc, z]
 
-        @pl.loop(0, NX)
+        @pl.loop(0, NX, unroll=True)
         def _(x):
             slot = slots[x * NZ + target, z]
             for kv in range(2):
@@ -372,12 +366,12 @@
         if onward == 0:
             pltpu.make_async_copy(stage.at[place, myx, myc], mine, recv.at[R_KV]).start()
 
-            @pl.loop(1, NX * NC)
+            @pl.loop(1, NX * NC, unroll=True)
             def _(k):
                 pages_to(lax.rem(myx + lax.div(k, NC), NX), lax.rem(myc + k, NC))
         elif len(cores) == 2:
 
-            @pl.loop(0, NX * NC)
+            @pl.loop(0, NX * NC, unroll=True)
             def _(k):
                 pages_to(lax.rem(myx + lax.div(k, NC), NX), lax.rem(myc + k, NC))
         else:
@@ -439,6 +433,13 @@
     for side in range(2):
         wait_for(bcbuf.at[myx, myc, far, map_rows(side)], ring_bc.at[side, 3])
     spread_maps(far)
+    @pl.loop(1, NDEV)
+    def _(step):
+        to = peer(step)
+        remote(
+            dt_stage.at[to], dtbuf.at[myz, myx, myc], send.at[S_DT], recv.at[R_DT], {"dev": to}
+        ).start()
+
     send_far()
     send_both_ways(3)
 

time: 108 us -> 107 us (level)
  no operation moved by 1% of the time
where the time goes in v2:
time: 107 us
  Pallas kernels  106 us (99%)
    pallas_call x1, Pallas kernels, on_device(): pl.pallas_call(kernel, out_shape=(pltpu.VMEM((REQ * NEW, 128), BF16), plt...  102 us
    pallas_call x1, Pallas kernels, on_device(): pl.pallas_call(hand_over, out_shape=tuple((jax.ShapeDtypeStruct(a.shape,...  4.34 us

profile of v2, /device:TPU:1, one launch (start us, length us, event | category | flops | bytes accessed | tf_op | source)
XLA Modules:
  0.0 106.8 jit_solution(1248577795689982783)
XLA Ops:
  0.6 0.0 copy-start
  0.6 0.0 copy-start.1
  0.7 101.8 %shard_map.139 = (bf16[8192,128]{1,0:T(8,128)(2,1)S(1)}, f32[32,128,128]{2,1,0:T(8,128)S(1)}, bf16[128,4096]{1,0:T(8,128)(2,1)S(1)}, bf16[8,4,2,128,128]{4,3,2,1...) custom-call(s32[32]{0:T(128)} %owners.3, f32[2]{0:T(128)} %a_log.1, ...), custom_call_target="tpu_custom_call" | custom-call | tf_op jit(solution)/shard_map/pallas_call | solution.py:636
  102.5 0.0 copy-done
  102.5 0.0 copy-done.1
  102.5 4.3 %shard_map.140 = (bf16[8192,128]{1,0:T(8,128)(2,1)}, f32[32,128,128]{2,1,0:T(8,128)}, bf16[128,4096]{1,0:T(8,128)(2,1)}) custom-call(s32[32]{0:T(128)S(1)} %copy-done, f32[2]{0:T(128)S(1)} %copy-done.1, bf16[8192,128]{1,0:T(8,128)(2,1)S(1)} %get-tuple-element.13.ssd_v, f32[32,128,128]{2,1,0:T(8,128)S(1)} %get-tuple-element.14.fin_v, ...), custom_call_target="tpu_custom_call" | custom-call | tf_op jit(solution)/shard_map/pallas_call | solution.py:688
Async XLA Ops:
  0.6 101.8 %copy-start = (s32[32]{0:T(128)S(1)}, s32[32]{0:T(128)}, u32[]{:S(2)}) copy-start(s32[32]{0:T(128)} %owners.3) | copy-start | bytes 388
  0.6 101.8 %copy-start.1 = (f32[2]{0:T(128)S(1)}, f32[2]{0:T(128)}, u32[]{:S(2)}) copy-start(f32[2]{0:T(128)} %d_skip.3) | copy-start | bytes 28
